TPU v7x, 128 devices: a whole 4x4x4 slice. The times are simulated.
128 devices in a mesh: node: 32 (over y, z, core), local: 4 (over x).
Axes of the slice: x: 4, y: 4, z: 4, core: 2. Of those that a mesh axis runs over, the one named last changes fastest.
Arguments:
- layer_input: bfloat16 [2048, 3584], P(('node', 'local')), may hold values from -6 to 6
- grad_output: bfloat16 [2048, 3584], P(('node', 'local')), may hold values from -6 to 6
- expert_ids: int32 [2048, 8], P(('node', 'local')), may hold values from 0 to 127, as said below
- route_weights: bfloat16 [2048, 8], P(('node', 'local')), may hold values from 0.099609375 to 1
- w_gate: bfloat16 [128, 3584, 1024], P(('node', 'local')), may hold values from -0.09375 to 0.09375
- w_up: bfloat16 [128, 3584, 1024], P(('node', 'local')), may hold values from -0.09375 to 0.09375
- w_down: bfloat16 [128, 1024, 3584], P(('node', 'local')), may hold values from -0.1875 to 0.1875
Outputs:
- input_grad: bfloat16 [2048, 3584], P(('node', 'local'))
Inputs may be any that keep to these rules, and one draw needn't show every extreme that they name: `expert_ids`: each row names 8 different experts, two in each of four different node groups, where expert e lies in node group e // 4 and is held by device e. Among the 16 tokens of one device at most 4 name a given node group, and in every device some group is named by exactly 4 of them; at most 2 name a given expert, and every device has an expert named exactly 2 times. Every expert is named by exactly 32 tokens of the devices of each local index, so by 128 tokens in all.
All inputs are finite; a program needn't handle non-finite values.
Results may differ from a plain program's by a relative error of at most 0.0049.
Values may be sent and summed in bfloat16 or wider, within the bound.
A program may use at most 128 MiB of HBM per device.

v0:
```python
import jax
import jax.numpy as jnp
from jax import lax
from jax.sharding import PartitionSpec as P


def expert_grad(packed_rows, scales, w_gate, w_up, w_down):
    in_width = w_gate.shape[0]
    inputs_part = packed_rows[:, :in_width]
    grads_part = packed_rows[:, in_width:]
    contract = (((1,), (1,)), ((), ()))
    pre_gate = jnp.dot(inputs_part, w_gate, preferred_element_type=jnp.float32)
    pre_up = jnp.dot(inputs_part, w_up, preferred_element_type=jnp.float32)
    hidden_grad = scales.astype(jnp.float32)[:, None] * lax.dot_general(
        grads_part, w_down, contract, preferred_element_type=jnp.float32
    )
    sigmoid_gate = jax.nn.sigmoid(pre_gate)
    d_gate = (hidden_grad * pre_up * sigmoid_gate * (1.0 + pre_gate * (1.0 - sigmoid_gate))).astype(
        jnp.bfloat16
    )
    d_up = (hidden_grad * pre_gate * sigmoid_gate).astype(jnp.bfloat16)
    return lax.dot_general(
        d_gate, w_gate, contract, preferred_element_type=jnp.float32
    ) + lax.dot_general(d_up, w_up, contract, preferred_element_type=jnp.float32)


def slot_sources(hit_table, capacity):
    slot_order = jnp.cumsum(hit_table, axis=0) - hit_table
    slot_ids = jnp.arange(capacity, dtype=jnp.int32)
    chosen = (hit_table.T[:, None, :] == 1) & (slot_order.T[:, None, :] == slot_ids[None, :, None])
    token_ids = jnp.arange(hit_table.shape[0], dtype=jnp.int32)
    sources = jnp.sum(jnp.where(chosen, token_ids[None, None, :], 0), axis=2)
    present = jnp.sum(chosen.astype(jnp.int32), axis=2)
    return (sources, present, chosen)


def local(layer_input, grad_output, expert_ids, route_weights, w_gate, w_up, w_down):
    tok_count = layer_input.shape[0]
    model_width = layer_input.shape[1]
    groups = lax.axis_size("node")
    local_count = lax.axis_size("local")
    devices = groups * local_count
    most_group = max(tok_count // 4, 4 * tok_count // groups)
    packed = jnp.concatenate([layer_input, grad_output], axis=1)
    onehot = expert_ids[:, :, None] == jnp.arange(devices, dtype=jnp.int32)[None, None, :]
    weights_te = jnp.sum(
        jnp.where(onehot, route_weights[:, :, None].astype(jnp.float32), 0.0), axis=1
    )
    empty_row = jnp.zeros((), jnp.bfloat16)
    pair_cap = most_group // 2
    hit_table = jnp.sum(onehot.astype(jnp.int32), axis=1)
    sources, present, chosen = slot_sources(hit_table, pair_cap)
    send_rows = jnp.where(present[..., None] > 0, packed[sources], empty_row)
    send_scales = jnp.sum(jnp.where(chosen, weights_te.T[:, None, :], 0.0), axis=2).astype(
        jnp.bfloat16
    )
    recv_rows, recv_scales = (
        lax.all_to_all(send_rows, ("node", "local"), split_axis=0, concat_axis=0, tiled=True),
        lax.all_to_all(send_scales, ("node", "local"), split_axis=0, concat_axis=0, tiled=True),
    )
    flat_rows = recv_rows.reshape(-1, recv_rows.shape[2])
    flat_scales = recv_scales.reshape(-1)
    is_live = (flat_scales > 0).astype(jnp.int32)[:, None]
    picked, _, _ = slot_sources(is_live, 8 * tok_count)
    picked = picked[0]
    grads_rows = expert_grad(flat_rows[picked], flat_scales[picked], w_gate[0], w_up[0], w_down[0])
    placed = jnp.zeros((flat_rows.shape[0], model_width), jnp.float32).at[picked].add(grads_rows)
    returned = lax.all_to_all(
        placed.reshape(devices, pair_cap, model_width),
        ("node", "local"),
        split_axis=0,
        concat_axis=0,
        tiled=True,
    )
    token_slots = jnp.where(present > 0, sources, tok_count)
    summed = (
        jnp.zeros((tok_count + 1, model_width), jnp.float32)
        .at[token_slots.reshape(-1)]
        .add(returned.reshape(-1, model_width))
    )
    return summed[:tok_count].astype(jnp.bfloat16)


def solution(mesh):
    return jax.shard_map(
        local,
        mesh=mesh,
        in_specs=(
            P(("node", "local"), None),
            P(("node", "local"), None),
            P(("node", "local"), None),
            P(("node", "local"), None),
            P(("node", "local"), None, None),
            P(("node", "local"), None, None),
            P(("node", "local"), None, None),
        ),
        out_specs=P(("node", "local"), None),
        check_vma=False,
    )
```

profile of v0, /device:TPU:1, one launch (start us, length us, event | category | flops | bytes accessed | tf_op | source)
XLA Modules:
  0.0 209.7 jit_solution(10223653816877151034)
XLA Ops:
  0.0 0.8 copy.25
  0.9 0.8 copy.27
  1.8 0.8 copy.28
  2.6 11.5 %all-to-all-start = ((bf16[128,1,2]{2,1,0:T(2,128)(2,1)}), bf16[128,1,2]{2,1,0:T(2,128)(2,1)S(1)}, u32[]{:S(2)}, u32[]{:S(2)}) async-start(bf16[128,1,2]{2,1,0:T(2,128)(2,1)} %copy.28), calls=%async_computation | async-start | bytes 131072 | tf_op jit(solution)/shard_map/all_to_all | solution.py:59
  14.4 1.0 pad_maximum_fusion
  15.4 4.7 %gather_fusion.1 = bf16[256,7168]{1,0:T(8,128)(2,1)} fusion(bf16[16,7168]{1,0:T(8,128)(2,1)S(1)} %pad_maximum_fusion, s32[1024]{0:T(1024)S(1)} %pad_clamp_fusion), kind=kCustom, calls=%fused_computation.1 | custom fusion | bytes 7341056 | tf_op jit(solution)/shard_map/gather | solution.py:53
  20.0 8.1 %reshape.269 = bf16[128,2,7168]{2,1,0:T(2,128)(2,1)} reshape(bf16[256,7168]{1,0:T(8,128)(2,1)} %gather_fusion.1) | data formatting | bytes 7340032 | tf_op jit(solution)/shard_map/gather | solution.py:53
  28.3 7.0 %broadcast_select_fusion = bf16[128,2,7168]{2,1,0:T(2,128)(2,1)} fusion(bf16[128,2,7168]{2,1,0:T(2,128)(2,1)} %reshape.269, pred[128,2]{1,0:T(8,128)(4,1)S(1)} %copy.29), kind=kLoop, calls=%fused_computation.15 | loop fusion | flops 1835008 | bytes 7340288 | tf_op jit(solution)/shard_map/jit(_where)/select_n | solution.py:53
  35.3 10.2 %all-to-all-start.1 = ((bf16[128,2,7168]{2,1,0:T(2,128)(2,1)}), bf16[128,2,7168]{2,1,0:T(2,128)(2,1)}, u32[]{:S(2)}, u32[]{:S(2)}) async-start(bf16[128,2,7168]{2,1,0:T(2,128)(2,1)} %broadcast_select_fusion), calls=%async_computation.1 | async-start | bytes 7340032 | tf_op jit(solution)/shard_map/all_to_all | solution.py:58
  47.1 1.2 gather_fusion
  48.3 44.7 %all-to-all-done.1 = bf16[128,2,7168]{2,1,0:T(2,128)(2,1)} async-done(((bf16[128,2,7168]{2,1,0:T(2,128)(2,1)}), bf16[128,2,7168]{2,1,0:T(2,128)(2,1)}, u32[]{:S(2)}, u32[]{:S(2)}) %all-to-all-start.1) | async-done | bytes 3670048 | tf_op jit(solution)/shard_map/all_to_all | solution.py:58
  93.0 8.4 %reshape.256 = bf16[256,7168]{1,0:T(8,128)(2,1)} reshape(bf16[128,2,7168]{2,1,0:T(2,128)(2,1)} %all-to-all-done.1) | data formatting | bytes 7340032 | tf_op jit(solution)/shard_map/reshape | solution.py:61
  101.4 5.9 %gather_fusion.2 = bf16[128,7168]{1,0:T(8,128)(2,1)S(1)} fusion(bf16[256,7168]{1,0:T(8,128)(2,1)} %reshape.256, s32[1024]{0:T(1024)S(1)} %pad_clamp_fusion.1), kind=kCustom, calls=%fused_computation.2 | custom fusion | bytes 3670528 | tf_op jit(solution)/shard_map/gather | solution.py:66
  107.3 4.2 %fusion.2 = f32[128,1024]{1,0:T(8,128)S(1)} fusion(bf16[1,3584,1024]{2,1,0:T(8,128)(2,1)} %param.11, bf16[128,7168]{1,0:T(8,128)(2,1)S(1)} %gather_fusion.2), kind=kOutput, calls=%fused_computation.7 | convolution fusion | flops 939524096 | bytes 8781824 | tf_op jit(solution)/shard_map/dot_general | solution.py:12
  111.5 5.6 %fusion.15 = f32[128,1024]{1,0:T(8,128)S(1)} fusion(bf16[1,1024,3584]{2,1,0:T(8,128)(2,1)} %param.13, bf16[128,7168]{1,0:T(8,128)(2,1)S(1)} %gather_fusion.2, f32[128]{0:T(128)S(1)} %convert_element_type.69), kind=kOutput, calls=%fused_computation.19 | convolution fusion | flops 939655168 | bytes 8782336 | tf_op jit(solution)/shard_map/dot_general | solution.py:14
  117.1 10.1 %fusion = f32[128,3584]{1,0:T(8,128)} fusion(bf16[1,3584,1024]{2,1,0:T(8,128)(2,1)} %param.11, f32[128,1024]{1,0:T(8,128)S(1)} %fusion.15, bf16[1,3584,1024]{2,1,0:T(8,128)(2,1)} %param.12, bf16[128,7168]{1,0:T(8,128)(2,1)S(1)} %gather_fusion.2, f32[128,1024]{1,0:T(8,128)S(1)} %fusion.2), kind=kOutput, calls=%fused_computation.5 | convolution fusion | flops 1880358912 | bytes 18481152 | tf_op jit(solution)/shard_map/dot_general | solution.py:22
  127.2 6.1 %fusion.10 = f32[128,3584]{1,0:T(8,128)S(1)} fusion(f32[128,3584]{1,0:T(8,128)} %fusion, bf16[1,3584,1024]{2,1,0:T(8,128)(2,1)} %param.12, f32[128,1024]{1,0:T(8,128)S(1)} %fusion.15, f32[128,1024]{1,0:T(8,128)S(1)} %fusion.2), kind=kOutput, calls=%fused_computation.16 | convolution fusion | flops 940769280 | bytes 12058624 | tf_op jit(solution)/shard_map/dot_general | solution.py:24
  133.3 5.2 %scatter_custom_fusion = f32[256,3584]{1,0:T(8,128)} fusion(s32[128]{0:T(128)S(1)} %fusion.49, f32[128,3584]{1,0:T(8,128)S(1)} %fusion.10, f32[]{:T(128)} %constant.8.clone.1), kind=kCustom, calls=%fused_computation.17 | custom fusion | flops 458752 | bytes 3670020 | tf_op jit(solution)/shard_map/scatter-add | solution.py:67
  138.4 5.6 %reshape.257 = f32[128,2,3584]{2,1,0:T(2,128)} reshape(f32[256,3584]{1,0:T(8,128)} %scatter_custom_fusion) | data formatting | bytes 7340032 | tf_op jit(solution)/shard_map/reshape | solution.py:69
  144.0 4.7 %all-to-all-start.2 = ((f32[128,2,3584]{2,1,0:T(2,128)}), f32[128,2,3584]{2,1,0:T(2,128)}, u32[]{:S(2)}, u32[]{:S(2)}) async-start(f32[128,2,3584]{2,1,0:T(2,128)} %reshape.257), calls=%async_computation.2 | async-start | bytes 7340032 | tf_op jit(solution)/shard_map/all_to_all | solution.py:68
  149.0 47.4 %all-to-all-done.2 = f32[128,2,3584]{2,1,0:T(2,128)} async-done(((f32[128,2,3584]{2,1,0:T(2,128)}), f32[128,2,3584]{2,1,0:T(2,128)}, u32[]{:S(2)}, u32[]{:S(2)}) %all-to-all-start.2) | async-done | bytes 3670048 | tf_op jit(solution)/shard_map/all_to_all | solution.py:68
  196.4 5.7 %reshape.296 = f32[256,3584]{1,0:T(8,128)} reshape(f32[128,2,3584]{2,1,0:T(2,128)} %all-to-all-done.2) | data formatting | bytes 7340032 | tf_op jit(solution)/shard_map/reshape | solution.py:79
  202.1 6.9 %scatter_custom_fusion.1 = f32[17,3584]{1,0:T(8,128)S(1)} fusion(s32[256]{0:T(256)S(1)} %bitcast.55, f32[256,3584]{1,0:T(8,128)} %reshape.296, f32[]{:T(128)} %constant.8.clone.1), kind=kCustom, calls=%fused_computation.37 | custom fusion | flops 917504 | bytes 244224 | tf_op jit(solution)/shard_map/scatter-add | solution.py:79
  209.0 0.7 slice.41
  (32 shorter events, 2.5 us)
Async XLA Ops:
  2.6 32.7 %all-to-all-start = ((bf16[128,1,2]{2,1,0:T(2,128)(2,1)}), bf16[128,1,2]{2,1,0:T(2,128)(2,1)S(1)}, u32[]{:S(2)}, u32[]{:S(2)}) async-start(bf16[128,1,2]{2,1,0:T(2,128)(2,1)} %copy.28), calls=%async_computation | async-start | bytes 131072 | tf_op jit(solution)/shard_map/all_to_all | solution.py:59
  35.3 57.7 %all-to-all-start.1 = ((bf16[128,2,7168]{2,1,0:T(2,128)(2,1)}), bf16[128,2,7168]{2,1,0:T(2,128)(2,1)}, u32[]{:S(2)}, u32[]{:S(2)}) async-start(bf16[128,2,7168]{2,1,0:T(2,128)(2,1)} %broadcast_select_fusion), calls=%async_computation.1 | async-start | bytes 7340032 | tf_op jit(solution)/shard_map/all_to_all | solution.py:58
  144.0 52.4 %all-to-all-start.2 = ((f32[128,2,3584]{2,1,0:T(2,128)}), f32[128,2,3584]{2,1,0:T(2,128)}, u32[]{:S(2)}, u32[]{:S(2)}) async-start(f32[128,2,3584]{2,1,0:T(2,128)} %reshape.257), calls=%async_computation.2 | async-start | bytes 7340032 | tf_op jit(solution)/shard_map/all_to_all | solution.py:68
where the time goes:
time: 211 us; the launch traced here: 210 us
  waiting for transfers between devices  92.1 us (44%)
  local copies, waits for them, and re-layouts  43.7 us (21%)
  starting transfers between devices  26.4 us (13%)
  matrix products  26 us (12%)
  other arithmetic  21.4 us (10%)
    all_to_all x1, waiting for transfers between devices, local(): lax.all_to_all(placed.reshape(devices, pair_cap, model_width), ('node', '...  47.4 us
    all_to_all x1, waiting for transfers between devices, local(): lax.all_to_all(send_rows, ('node', 'local'), split_axis=0, concat_axis=0,...  44.7 us
    gather x2, local copies, waits for them, and re-layouts, local(): send_rows = jnp.where(present[..., None] > 0, packed[sources], empty_row)  12.8 us
    all_to_all x1, starting transfers between devices, local(): lax.all_to_all(send_scales, ('node', 'local'), split_axis=0, concat_axis=...  11.5 us
    all_to_all x1, starting transfers between devices, local(): lax.all_to_all(send_rows, ('node', 'local'), split_axis=0, concat_axis=0,...  10.2 us
    dot_general x1, matrix products, expert_grad(): lax.dot_general(d_gate, w_gate, contract, preferred_element_type=jnp.floa...  10.1 us
    reshape x1, local copies, waits for them, and re-layouts, local(): flat_rows = recv_rows.reshape(-1, recv_rows.shape[2])  8.4 us
    select_n x2, other arithmetic, local(): send_rows = jnp.where(present[..., None] > 0, packed[sources], empty_row)  7 us
  transfers between devices with their start and end apart: 3, of which 2 were waited for; matrix products, arithmetic and copies ran while one was open for 12% of the time, Pallas kernels for 0%

commit v1 on v0

v1 whole, which is shorter than its diff:
```python
import jax
import jax.numpy as jnp
from jax import lax
from jax.experimental import pallas as pl
from jax.experimental.pallas import tpu as pltpu
from jax.sharding import PartitionSpec as P

MESH = pl.DeviceIdType.MESH
BF16 = jnp.bfloat16
F32 = jnp.float32

D = 3584
HW = 1024
TOK = 16
OUT_CUTS = (768, 1024, 1024, 768)
BACK_CUTS = (1024, 1024, 768, 768)
NB = 256


def pieces(cuts):
    starts = [sum(cuts[:i]) for i in range(len(cuts))]
    return tuple(zip(starts, cuts))


OUT_PIECES = pieces(OUT_CUTS)
BACK_PIECES = pieces(BACK_CUTS)


def iota(shape, dim):
    return lax.broadcasted_iota(jnp.int32, shape, dim)


def dot(a, b):
    return jnp.dot(a, b, preferred_element_type=F32)


def dot_t(a, b):
    return lax.dot_general(a, b, (((1,), (1,)), ((), ())), preferred_element_type=F32)


def as01(mask):
    return jnp.where(mask, 1.0, 0.0).astype(BF16)


def rows(start, size):
    return pl.ds(pl.multiple_of(start, size), size)


def kernel(
    x_in,
    g_in,
    ids,
    route,
    wg_hbm,
    wu_hbm,
    wd_hbm,
    out,
    wg,
    wu,
    wd,
    w_tok,
    m1,
    m2,
    m_s,
    m_r,
    mx_s,
    mx_r,
    a1,
    a2,
    s1,
    s2,
    r1,
    r2,
    x_s,
    x_r,
    sel1,
    sel2,
    sel1t,
    sel2t,
    pick1,
    pick2,
    pick1t,
    pick2t,
    pre_gate,
    pre_up,
    hidden,
    d_gate,
    d_up,
    y_s,
    y_r,
    u_s,
    u_r,
    q_s,
    q_r,
    w_sem,
    meta_sem,
    h1_sem,
    h2_sem,
    x_sem,
    b1_sem,
    b2_sem,
    b3_sem,
    send_sem,
):
    node = lax.axis_index("node")
    xi = lax.axis_index("local")
    yi, zi, ci = node // 8, lax.rem(node // 2, 4), lax.rem(node, 2)

    def turn(v, k, size):
        return lax.rem(v + k, size)

    def device(y, z, c, x):
        return (y * 8 + z * 2 + c, x)

    far_first = (2, 1, 3)
    y_line = [(turn(yi, k, 4), device(turn(yi, k, 4), zi, ci, xi)) for k in far_first]
    z_line = [(turn(zi, k, 4), device(yi, turn(zi, k, 4), ci, xi)) for k in far_first]
    x_line = [(turn(xi, k, 4), device(yi, zi, ci, turn(xi, k, 4))) for k in far_first]
    steps = [(k, c) for k in far_first for c in (0, 1)] + [(0, 1)]
    zc_plane = [
        (turn(zi, k, 4) * 2 + turn(ci, c, 2), device(yi, turn(zi, k, 4), turn(ci, c, 2), xi))
        for k, c in steps
    ]
    yc_plane = [
        (turn(yi, k, 4) * 2 + turn(ci, c, 2), device(turn(yi, k, 4), zi, turn(ci, c, 2), xi))
        for k, c in steps
    ]
    lines = (y_line, z_line)
    planes = (zc_plane, yc_plane)
    line_at = (yi, zi)
    plane_at = (zi * 2 + ci, yi * 2 + ci)

    def local_copy(src, dst, sem):
        pltpu.make_async_copy(src, dst, sem).start()

    def remote_copy(src, dst, sem, send, target):
        pltpu.make_async_remote_copy(
            src_ref=src,
            dst_ref=dst,
            send_sem=send_sem.at[send],
            recv_sem=sem,
            device_id=target,
            device_id_type=MESH,
        ).start()

    def await_bytes(ref, sem):
        pltpu.make_async_copy(ref, ref, sem).wait()

    def weight_copies(i):
        start, width = OUT_PIECES[i]
        cut = pl.ds(start, width)
        return (
            pltpu.make_async_copy(wg_hbm.at[0, cut, :], wg.at[cut, :], w_sem.at[0, i]),
            pltpu.make_async_copy(wu_hbm.at[0, cut, :], wu.at[cut, :], w_sem.at[1, i]),
            pltpu.make_async_copy(wd_hbm.at[0, :, cut], wd.at[:, cut], w_sem.at[2, i]),
        )

    barrier = pltpu.get_barrier_semaphore()
    partners = [d for _, d in zc_plane] + [d for _, d in yc_plane[:-1]] + [d for _, d in x_line]
    for target in partners:
        pl.semaphore_signal(barrier, inc=1, device_id=target, device_id_type=MESH)

    lane = iota((TOK, 128), 1)
    table = jnp.zeros((TOK, 128), F32)
    id_block, route_block = ids[...], route[...].astype(F32)
    for k in range(8):
        table += jnp.where(id_block[:, k : k + 1] == lane, route_block[:, k : k + 1], 0.0)
    w_tok[...] = table.astype(BF16)

    pl.semaphore_wait(barrier, len(partners))

    metas = (m1, m2)
    gathered = (a1, a2)
    sources = (x_in, g_in)
    spread_s, spread_r = (s1, s2), (r1, r2)
    sel, sel_t = (sel1, sel2), (sel1t, sel2t)
    pick, pick_t = (pick1, pick2), (pick1t, pick2t)

    for p in (0, 1):
        mine = metas[p].at[rows(line_at[p] * TOK, TOK), :]
        for _, target in lines[p]:
            remote_copy(w_tok, mine, meta_sem.at[p], p, target)
        local_copy(w_tok, mine, meta_sem.at[p])

    def gather(i):
        start, width = OUT_PIECES[i]
        cut = pl.ds(start, width)
        for p in (0, 1):
            mine = gathered[p].at[rows(line_at[p] * TOK, TOK), cut]
            for _, target in lines[p]:
                remote_copy(sources[p].at[:, cut], mine, h1_sem.at[p, i], 4 + p, target)
            local_copy(sources[p].at[:, cut], mine, h1_sem.at[p, i])

    def spread(i):
        start, width = OUT_PIECES[i]
        cut = pl.ds(start, width)
        for p in (0, 1):
            await_bytes(gathered[p].at[:, cut], h1_sem.at[p, i])
            spread_s[p][:, cut] = dot(sel[p][...], gathered[p][:, cut]).astype(BF16)
            mine = rows(plane_at[p] * TOK, TOK)
            for at, target in planes[p]:
                remote_copy(
                    spread_s[p].at[rows(at * TOK, TOK), cut],
                    spread_r[p].at[mine, cut],
                    h2_sem.at[p, i],
                    6 + p,
                    target,
                )
            local_copy(spread_s[p].at[mine, cut], spread_r[p].at[mine, cut], h2_sem.at[p, i])

    def forward(i):
        start, width = OUT_PIECES[i]
        cut = pl.ds(start, width)
        for p in (0, 1):
            await_bytes(spread_r[p].at[:, cut], h2_sem.at[p, i])
            x_s[:, pl.ds(2 * start + p * width, width)] = dot(
                pick[p][...], spread_r[p][:, cut]
            ).astype(BF16)
        both = pl.ds(2 * start, 2 * width)
        mine = rows(xi * 32, 32)
        for at, target in x_line:
            remote_copy(x_s.at[rows(at * 32, 32), both], x_r.at[mine, both], x_sem.at[i], 8, target)
        local_copy(x_s.at[mine, both], x_r.at[mine, both], x_sem.at[i])

    def multiply(i):
        start, width = OUT_PIECES[i]
        cut = pl.ds(start, width)
        both = pl.ds(2 * start, 2 * width)
        for copy in weight_copies(i):
            copy.wait()
        await_bytes(x_r.at[:, both], x_sem.at[i])
        x_part = x_r[:, pl.ds(2 * start, width)]
        g_part = x_r[:, pl.ds(2 * start + width, width)]

        @pl.loop(0, HW // NB)
        def _(n):
            block = rows(n * NB, NB)
            gate = dot(x_part, wg[cut, block])
            up = dot(x_part, wu[cut, block])
            hid = dot_t(g_part, wd[block, cut])
            if i == 0:
                pre_gate[:, block] = gate
                pre_up[:, block] = up
                hidden[:, block] = hid
            else:
                pre_gate[:, block] += gate
                pre_up[:, block] += up
                hidden[:, block] += hid

    def choose_tokens():
        row, col = iota((128, 128), 0), iota((128, 128), 1)
        group = col >> 2
        named = (
            ((group >> 3) == yi) & ((group & 7) == (row >> 4)),
            (((group >> 1) & 3) == zi) & (((group >> 3) * 2 + (group & 1)) == (row >> 4)),
        )
        t0, t1 = iota((64, 64), 0), iota((64, 64), 1)
        same = (t0 >> 4) == (t1 >> 4)
        before, after = as01(same & (t0 < t1)), as01(same & (t1 < t0))
        r0, c0 = iota((128, 64), 0), iota((128, 64), 1)
        r1_, c1_ = iota((64, 128), 0), iota((64, 128), 1)
        for p in (0, 1):
            await_bytes(metas[p], meta_sem.at[p])
            hits = as01(metas[p][...].astype(F32) > 0)
            want = as01(named[p])
            hit = dot_t(want, hits) > 0.5
            rank = dot(as01(hit), before).astype(jnp.int32)
            ok = hit & (((r0 >> 2) & 3) == (c0 >> 4)) & ((r0 & 3) == rank)
            sel[p][...] = as01(ok)
            hit_t = dot_t(hits, want) > 0.5
            rank_t = dot(after, as01(hit_t)).astype(jnp.int32)
            ok_t = hit_t & (((c1_ >> 2) & 3) == (r1_ >> 4)) & ((c1_ & 3) == rank_t)
            sel_t[p][...] = as01(ok_t)
        m_s[...] = dot(sel1[...], m1[...]).astype(BF16)
        mine = rows(plane_at[0] * TOK, TOK)
        for at, target in planes[0]:
            remote_copy(m_s.at[rows(at * TOK, TOK), :], m_r.at[mine, :], meta_sem.at[2], 2, target)
        local_copy(m_s.at[mine, :], m_r.at[mine, :], meta_sem.at[2])

    def choose_slots():
        row, col = iota((128, 128), 0), iota((128, 128), 1)
        await_bytes(m_r, meta_sem.at[2])
        hits = as01(m_r[...].astype(F32) > 0)
        want = as01(col == node * 4 + (row >> 5))
        hit = dot_t(want, hits) > 0.5
        rank = dot(as01(hit), as01(row < col)).astype(jnp.int32)
        p1 = as01(hit & (rank == (row & 31)))
        pick1[...] = p1
        hit_t = dot_t(hits, want) > 0.5
        rank_t = dot(as01(col < row), as01(hit_t)).astype(jnp.int32)
        p1t = as01(hit_t & (rank_t == (col & 31)))
        pick1t[...] = p1t
        moved = ((row >> 2) & 3) * 32 + (row & 16) + (row >> 5) * 4 + (row & 3)
        swap = as01(moved == col)
        pick2[...] = dot(p1, swap).astype(BF16)
        pick2t[...] = dot(swap, p1t).astype(BF16)
        mx_s[...] = dot(p1, m_r[...]).astype(BF16)
        mine = rows(xi * 32, 32)
        for at, target in x_line:
            remote_copy(mx_s.at[rows(at * 32, 32), :], mx_r.at[mine, :], meta_sem.at[3], 3, target)
        local_copy(mx_s.at[mine, :], mx_r.at[mine, :], meta_sem.at[3])

    def activate():
        await_bytes(mx_r, meta_sem.at[3])
        scale = jnp.sum(
            jnp.where(iota((128, 128), 1) == node * 4 + xi, mx_r[...].astype(F32), 0.0),
            axis=1,
            keepdims=True,
        )

        @pl.loop(0, HW // NB)
        def _(n):
            block = rows(n * NB, NB)
            gate, up = pre_gate[:, block], pre_up[:, block]
            grad = scale * hidden[:, block]
            s = jax.nn.sigmoid(gate)
            d_gate[:, block] = (grad * up * s * (1.0 + gate * (1.0 - s))).astype(BF16)
            d_up[:, block] = (grad * gate * s).astype(BF16)

    def back_rows(i):
        start, width = BACK_PIECES[i]
        cut = pl.ds(start, width)

        @pl.loop(0, width // NB)
        def _(n):
            block = rows(start + n * NB, NB)
            total = dot_t(d_gate[...], wg[block, :]) + dot_t(d_up[...], wu[block, :])
            y_s[:, block] = total.astype(BF16)

        mine = rows(xi * 32, 32)
        for at, target in x_line:
            remote_copy(y_s.at[rows(at * 32, 32), cut], y_r.at[mine, cut], b1_sem.at[i], 9, target)
        local_copy(y_s.at[mine, cut], y_r.at[mine, cut], b1_sem.at[i])

    def back_slots(i):
        start, width = BACK_PIECES[i]
        cut = pl.ds(start, width)
        p = i % 2
        await_bytes(y_r.at[:, cut], b1_sem.at[i])
        u_s[:, cut] = dot(pick_t[p][...], y_r[:, cut]).astype(BF16)
        mine = rows(plane_at[p] * TOK, TOK)
        for at, target in planes[p]:
            remote_copy(
                u_s.at[rows(at * TOK, TOK), cut], u_r.at[mine, cut], b2_sem.at[i], 10, target
            )
        local_copy(u_s.at[mine, cut], u_r.at[mine, cut], b2_sem.at[i])

    def back_tokens(i):
        start, width = BACK_PIECES[i]
        cut = pl.ds(start, width)
        p = i % 2
        await_bytes(u_r.at[:, cut], b2_sem.at[i])
        q_s[:, cut] = dot(sel_t[p][...], u_r[:, cut]).astype(BF16)
        mine = rows(line_at[p] * TOK, TOK)
        for at, target in lines[p]:
            remote_copy(
                q_s.at[rows(at * TOK, TOK), cut], q_r.at[mine, cut], b3_sem.at[i], 11, target
            )
        local_copy(q_s.at[mine, cut], q_r.at[mine, cut], b3_sem.at[i])

    def finish(i):
        start, width = BACK_PIECES[i]
        cut = pl.ds(start, width)
        await_bytes(q_r.at[:, cut], b3_sem.at[i])
        total = q_r[0:TOK, cut].astype(F32)
        for k in range(1, 4):
            total += q_r[k * TOK : (k + 1) * TOK, cut].astype(F32)
        out[:, cut] = total.astype(BF16)

    count = len(OUT_PIECES)
    gather(0)
    for i in range(count):
        for copy in weight_copies(i):
            copy.start()
    gather(1)
    choose_tokens()
    for s in range(count + 2):
        if s < count:
            spread(s)
            if s + 2 < count:
                gather(s + 2)
        if s == 0:
            choose_slots()
        if 0 <= s - 1 < count:
            forward(s - 1)
        if 0 <= s - 2 < count:
            multiply(s - 2)
    activate()
    count = len(BACK_PIECES)
    for s in range(count + 3):
        if s < count:
            back_rows(s)
        if 0 <= s - 1 < count:
            back_slots(s - 1)
        if 0 <= s - 2 < count:
            back_tokens(s - 2)
        if 0 <= s - 3 < count:
            finish(s - 3)

    for p in (0, 1):
        await_bytes(metas[p].at[0:48, :], send_sem.at[p])
        await_bytes(gathered[p].at[0:48, :], send_sem.at[4 + p])
        await_bytes(spread_s[p].at[0:112, :], send_sem.at[6 + p])
    await_bytes(m_s.at[0:112, :], send_sem.at[2])
    await_bytes(mx_s.at[0:96, :], send_sem.at[3])
    await_bytes(x_s.at[0:96, :], send_sem.at[8])
    await_bytes(y_s.at[0:96, :], send_sem.at[9])
    await_bytes(u_s.at[0:112, :], send_sem.at[10])
    await_bytes(q_s.at[0:48, :], send_sem.at[11])


def local(layer_input, grad_output, expert_ids, route_weights, w_gate, w_up, w_down):
    vmem = pl.BlockSpec(memory_space=pltpu.VMEM)
    anywhere = pl.BlockSpec(memory_space=pl.ANY)
    dma = pltpu.SemaphoreType.DMA
    n_out, n_back = len(OUT_PIECES), len(BACK_PIECES)

    def buf(*shape):
        return pltpu.VMEM(shape, BF16)

    scratch = [
        buf(D, HW),
        buf(D, HW),
        buf(HW, D),
        buf(TOK, 128),
        buf(64, 128),
        buf(64, 128),
        buf(128, 128),
        buf(128, 128),
        buf(128, 128),
        buf(128, 128),
        buf(64, D),
        buf(64, D),
        buf(128, D),
        buf(128, D),
        buf(128, D),
        buf(128, D),
        buf(128, 2 * D),
        buf(128, 2 * D),
        buf(128, 64),
        buf(128, 64),
        buf(64, 128),
        buf(64, 128),
        buf(128, 128),
        buf(128, 128),
        buf(128, 128),
        buf(128, 128),
        pltpu.VMEM((128, HW), F32),
        pltpu.VMEM((128, HW), F32),
        pltpu.VMEM((128, HW), F32),
        buf(128, HW),
        buf(128, HW),
        buf(128, D),
        buf(128, D),
        buf(128, D),
        buf(128, D),
        buf(64, D),
        buf(64, D),
        dma((3, n_out)),
        dma((4,)),
        dma((2, n_out)),
        dma((2, n_out)),
        dma((n_out,)),
        dma((n_back,)),
        dma((n_back,)),
        dma((n_back,)),
        dma((12,)),
    ]
    return pl.pallas_call(
        kernel,
        out_shape=jax.ShapeDtypeStruct((TOK, D), BF16),
        in_specs=[anywhere, anywhere, vmem, vmem, anywhere, anywhere, anywhere],
        out_specs=vmem,
        scratch_shapes=scratch,
        compiler_params=pltpu.CompilerParams(
            collective_id=0, has_side_effects=True, vmem_limit_bytes=60 * 2**20
        ),
    )(layer_input, grad_output, expert_ids, route_weights, w_gate, w_up, w_down)


def solution(mesh):
    both = ("node", "local")
    return jax.shard_map(
        local,
        mesh=mesh,
        in_specs=(
            P(both, None),
            P(both, None),
            P(both, None),
            P(both, None),
            P(both, None, None),
            P(both, None, None),
            P(both, None, None),
        ),
        out_specs=P(both, None),
        check_vma=False,
    )
```

time: 211 us -> 76.9 us (0.36)
  waiting for transfers between devices: 92.1 us -> 0 us
  Pallas kernels: 0 us -> 72.4 us
  local copies, waits for them, and re-layouts: 43.7 us -> 4.25 us
  starting transfers between devices: 26.4 us -> 0 us
  matrix products: 26 us -> 0 us
  other arithmetic: 21.4 us -> 0 us
    all_to_all x3 -> x0, waiting for transfers between devices: 92.1 us -> none  [the longest x1 47.4 us: local(): lax.all_to_all(placed.reshape(devices, pair_cap, model_width), ('node', '...]
    pallas_call x0 -> x1, Pallas kernels: none -> 72.4 us  [local(): pl.pallas_call(kernel, out_shape=jax.ShapeDtypeStruct((TOK, D), BF16), in...]
    all_to_all x3 -> x0, starting transfers between devices: 26.4 us -> none  [the longest x1 11.5 us: local(): lax.all_to_all(send_scales, ('node', 'local'), split_axis=0, concat_axis=...]
    dot_general x4 -> x0, matrix products: 26 us -> none  [the longest x1 10.1 us: expert_grad(): lax.dot_general(d_gate, w_gate, contract, preferred_element_type=jnp.floa...]
    gather x4 -> x0, local copies, waits for them, and re-layouts: 19.9 us -> none  [the longest x2 12.8 us: local(): send_rows = jnp.where(present[..., None] > 0, packed[sources], empty_row)]
    reshape x4 -> x0, local copies, waits for them, and re-layouts: 19.8 us -> none  [the longest x1 8.4 us: local(): flat_rows = recv_rows.reshape(-1, recv_rows.shape[2])]
    scatter-add x2 -> x0, other arithmetic: 12 us -> none  [the longest x1 6.88 us: local(): summed = jnp.zeros((tok_count + 1, model_width), jnp.float32).at[token_sl...]
    select_n x5 -> x0, other arithmetic: 7.02 us -> none  [the longest x2 7 us: local(): send_rows = jnp.where(present[..., None] > 0, packed[sources], empty_row)]
  transfers between devices with their start and end apart: 3 -> 0, of which waited for: 2 -> 0; matrix products, arithmetic and copies ran while one was open for 12% -> 0% of each run, Pallas kernels for 0% -> 0%
where the time goes in v1:
time: 76.9 us; the launch traced here: 76.7 us
  Pallas kernels  72.4 us (94%)
  local copies, waits for them, and re-layouts  4.25 us (6%)
    pallas_call x1, Pallas kernels, local(): pl.pallas_call(kernel, out_shape=jax.ShapeDtypeStruct((TOK, D), BF16), in...  72.4 us
    unnamed x3, local copies, waits for them, and re-layouts  4.25 us

profile of v1, /device:TPU:1, one launch (start us, length us, event | category | flops | bytes accessed | tf_op | source)
XLA Modules:
  0.0 76.7 jit_solution(1460448516344600257)
XLA Ops:
  0.0 1.3 %copy.9.route = bf16[16,8]{1,0:T(8,128)(2,1)} copy(bf16[16,8]{0,1:T(8,128)(2,1)} %param.10) | data formatting | bytes 512 | tf_op args[3]
  1.3 1.4 %copy.8.ids = s32[16,8]{1,0:T(8,128)} copy(s32[16,8]{0,1:T(8,128)} %param.9) | data formatting | bytes 1024 | tf_op args[2]
  2.7 72.4 %shard_map.73 = bf16[16,3584]{1,0:T(8,128)(2,1)} custom-call(bf16[16,3584]{1,0:T(8,128)(2,1)} %x_in.1, bf16[16,3584]{1,0:T(8,128)(2,1)} %g_in.1, s32[16,8]{1,0:T(8,128)} %copy.8.ids, bf16[16,8]{1,0:T(8,128)(2,1)} %copy.9.route, bf16[1,3584,1024]{2,1,0:T(8,128)(2,1)} %wg_hbm.1, bf16[1,3584,1024]{2,1,0:T(8,128)(2,1)} %wu_hbm.1, bf16[1,1024,3584]{2,1,0:T(8,128)(2,1)} %wd_hbm.1), custom_call_target="tpu_custom_call" | custom-call | tf_op jit(solution)/shard_map/pallas_call | solution.py:469
  75.1 1.6 %copy.11 = bf16[16,3584]{1,0:T(8,128)(2,1)} copy(bf16[16,3584]{1,0:T(8,128)(2,1)} %shard_map.73) | data formatting | bytes 229376

commit v2 on v1

--- a/solution.py
+++ b/solution.py
@@ -12,8 +12,9 @@
 D = 3584
 HW = 1024
 TOK = 16
-OUT_CUTS = (768, 1024, 1024, 768)
-BACK_CUTS = (1024, 1024, 768, 768)
+OUT_CUTS = (512, 768, 768, 768, 512, 256)
+BACK_CUTS = (512,) * 7
+HB = 512
 NB = 256
 
 
@@ -24,6 +25,18 @@
 
 OUT_PIECES = pieces(OUT_CUTS)
 BACK_PIECES = pieces(BACK_CUTS)
+
+
+OUT_LAGS = (-3, 0, 2, 4)
+BACK_LAGS = (0, 4, 7, 10)
+
+
+def run_in_order(count, stages, lags, before):
+    order = sorted((i + lag, k, i) for k, lag in enumerate(lags) for i in range(count))
+    for _, k, i in order:
+        if (i, k) in before:
+            before[(i, k)]()
+        stages[k](i)
 
 
 def iota(shape, dim):
@@ -54,7 +67,7 @@
     wg_hbm,
     wu_hbm,
     wd_hbm,
-    out,
+    q_r,
     wg,
     wu,
     wd,
@@ -81,6 +94,9 @@
     pick2,
     pick1t,
     pick2t,
+    want1,
+    want2,
+    want_x,
     pre_gate,
     pre_up,
     hidden,
@@ -91,7 +107,6 @@
     u_s,
     u_r,
     q_s,
-    q_r,
     w_sem,
     meta_sem,
     h1_sem,
@@ -160,12 +175,30 @@
     for target in partners:
         pl.semaphore_signal(barrier, inc=1, device_id=target, device_id_type=MESH)
 
-    lane = iota((TOK, 128), 1)
-    table = jnp.zeros((TOK, 128), F32)
+    for i in range(len(OUT_PIECES)):
+        for copy in weight_copies(i):
+            copy.start()
+
+    down = iota((128, TOK), 0)
+    table_t = jnp.zeros((128, TOK), F32)
     id_block, route_block = ids[...], route[...].astype(F32)
     for k in range(8):
-        table += jnp.where(id_block[:, k : k + 1] == lane, route_block[:, k : k + 1], 0.0)
-    w_tok[...] = table.astype(BF16)
+        table_t += jnp.where(id_block[k : k + 1, :] == down, route_block[k : k + 1, :], 0.0)
+    small0, small1 = iota((TOK, TOK), 0), iota((TOK, TOK), 1)
+    table = dot_t(as01(small0 == small1), table_t.astype(BF16))
+    row, col = iota((128, 128), 0), iota((128, 128), 1)
+    in_group = dot(as01(table > 0), as01((row >> 2) == (col >> 2))) > 0.5
+    rank = dot(as01(small1 < small0), as01(in_group))
+    w_tok[:, 0:128] = table.astype(BF16)
+    w_tok[:, 128:256] = jnp.where(in_group, rank + 1.0, 0.0).astype(BF16)
+    first = (col & 3) == 0
+    group = col >> 2
+    place = row >> 4
+    want1[...] = as01(first & ((group >> 3) == yi) & ((group & 7) == place))
+    want2[...] = as01(
+        first & (((group >> 1) & 3) == zi) & (((group >> 3) * 2 + (group & 1)) == place)
+    )
+    want_x[...] = as01(col == node * 4 + (row >> 5))
 
     pl.semaphore_wait(barrier, len(partners))
 
@@ -175,6 +208,7 @@
     spread_s, spread_r = (s1, s2), (r1, r2)
     sel, sel_t = (sel1, sel2), (sel1t, sel2t)
     pick, pick_t = (pick1, pick2), (pick1t, pick2t)
+    wants = (want1, want2)
 
     for p in (0, 1):
         mine = metas[p].at[rows(line_at[p] * TOK, TOK), :]
@@ -232,9 +266,9 @@
         x_part = x_r[:, pl.ds(2 * start, width)]
         g_part = x_r[:, pl.ds(2 * start + width, width)]
 
-        @pl.loop(0, HW // NB)
+        @pl.loop(0, HW // HB)
         def _(n):
-            block = rows(n * NB, NB)
+            block = rows(n * HB, HB)
             gate = dot(x_part, wg[cut, block])
             up = dot(x_part, wu[cut, block])
             hid = dot_t(g_part, wd[block, cut])
@@ -248,30 +282,15 @@
                 hidden[:, block] += hid
 
     def choose_tokens():
-        row, col = iota((128, 128), 0), iota((128, 128), 1)
-        group = col >> 2
-        named = (
-            ((group >> 3) == yi) & ((group & 7) == (row >> 4)),
-            (((group >> 1) & 3) == zi) & (((group >> 3) * 2 + (group & 1)) == (row >> 4)),
-        )
-        t0, t1 = iota((64, 64), 0), iota((64, 64), 1)
-        same = (t0 >> 4) == (t1 >> 4)
-        before, after = as01(same & (t0 < t1)), as01(same & (t1 < t0))
         r0, c0 = iota((128, 64), 0), iota((128, 64), 1)
-        r1_, c1_ = iota((64, 128), 0), iota((64, 128), 1)
+        fits = ((r0 >> 2) & 3) == (c0 >> 4)
+        slot = ((r0 & 3) + 1).astype(F32)
         for p in (0, 1):
             await_bytes(metas[p], meta_sem.at[p])
-            hits = as01(metas[p][...].astype(F32) > 0)
-            want = as01(named[p])
-            hit = dot_t(want, hits) > 0.5
-            rank = dot(as01(hit), before).astype(jnp.int32)
-            ok = hit & (((r0 >> 2) & 3) == (c0 >> 4)) & ((r0 & 3) == rank)
-            sel[p][...] = as01(ok)
-            hit_t = dot_t(hits, want) > 0.5
-            rank_t = dot(after, as01(hit_t)).astype(jnp.int32)
-            ok_t = hit_t & (((c1_ >> 2) & 3) == (r1_ >> 4)) & ((c1_ & 3) == rank_t)
-            sel_t[p][...] = as01(ok_t)
-        m_s[...] = dot(sel1[...], m1[...]).astype(BF16)
+        for p in (0, 1):
+            found = dot_t(wants[p][...], metas[p][:, 128:256])
+            sel[p][...] = as01(fits & (found == slot))
+        m_s[...] = dot(sel1[...], m1[:, 0:128]).astype(BF16)
         mine = rows(plane_at[0] * TOK, TOK)
         for at, target in planes[0]:
             remote_copy(m_s.at[rows(at * TOK, TOK), :], m_r.at[mine, :], meta_sem.at[2], 2, target)
@@ -281,24 +300,28 @@
         row, col = iota((128, 128), 0), iota((128, 128), 1)
         await_bytes(m_r, meta_sem.at[2])
         hits = as01(m_r[...].astype(F32) > 0)
-        want = as01(col == node * 4 + (row >> 5))
-        hit = dot_t(want, hits) > 0.5
+        hit = dot_t(want_x[...], hits) > 0.5
         rank = dot(as01(hit), as01(row < col)).astype(jnp.int32)
         p1 = as01(hit & (rank == (row & 31)))
         pick1[...] = p1
-        hit_t = dot_t(hits, want) > 0.5
-        rank_t = dot(as01(col < row), as01(hit_t)).astype(jnp.int32)
-        p1t = as01(hit_t & (rank_t == (col & 31)))
-        pick1t[...] = p1t
-        moved = ((row >> 2) & 3) * 32 + (row & 16) + (row >> 5) * 4 + (row & 3)
-        swap = as01(moved == col)
-        pick2[...] = dot(p1, swap).astype(BF16)
-        pick2t[...] = dot(swap, p1t).astype(BF16)
-        mx_s[...] = dot(p1, m_r[...]).astype(BF16)
+        pick2[...] = dot(p1, as01(swapped(row) == col)).astype(BF16)
+
+    def swapped(slot):
+        return ((slot >> 2) & 3) * 32 + (slot & 16) + (slot >> 5) * 4 + (slot & 3)
+
+    def choose_late():
+        mx_s[...] = dot(pick1[...], m_r[...]).astype(BF16)
         mine = rows(xi * 32, 32)
         for at, target in x_line:
             remote_copy(mx_s.at[rows(at * 32, 32), :], mx_r.at[mine, :], meta_sem.at[3], 3, target)
         local_copy(mx_s.at[mine, :], mx_r.at[mine, :], meta_sem.at[3])
+        row, col = iota((128, 128), 0), iota((128, 128), 1)
+        same = as01(row == col)
+        p1t = dot_t(same, pick1[...]).astype(BF16)
+        pick1t[...] = p1t
+        pick2t[...] = dot(as01(swapped(row) == col), p1t).astype(BF16)
+        for p in (0, 1):
+            sel_t[p][...] = dot_t(same[0:64, 0:64], sel[p][...]).astype(BF16)
 
     def activate():
         await_bytes(mx_r, meta_sem.at[3])
@@ -360,42 +383,16 @@
 
     def finish(i):
         start, width = BACK_PIECES[i]
-        cut = pl.ds(start, width)
-        await_bytes(q_r.at[:, cut], b3_sem.at[i])
-        total = q_r[0:TOK, cut].astype(F32)
-        for k in range(1, 4):
-            total += q_r[k * TOK : (k + 1) * TOK, cut].astype(F32)
-        out[:, cut] = total.astype(BF16)
-
-    count = len(OUT_PIECES)
-    gather(0)
-    for i in range(count):
-        for copy in weight_copies(i):
-            copy.start()
-    gather(1)
-    choose_tokens()
-    for s in range(count + 2):
-        if s < count:
-            spread(s)
-            if s + 2 < count:
-                gather(s + 2)
-        if s == 0:
-            choose_slots()
-        if 0 <= s - 1 < count:
-            forward(s - 1)
-        if 0 <= s - 2 < count:
-            multiply(s - 2)
+        await_bytes(q_r.at[:, pl.ds(start, width)], b3_sem.at[i])
+
+    out_extra = {
+        (0, 1): choose_tokens,
+        (0, 2): choose_slots,
+        (0, 3): choose_late,
+    }
+    run_in_order(len(OUT_PIECES), (gather, spread, forward, multiply), OUT_LAGS, out_extra)
     activate()
-    count = len(BACK_PIECES)
-    for s in range(count + 3):
-        if s < count:
-            back_rows(s)
-        if 0 <= s - 1 < count:
-            back_slots(s - 1)
-        if 0 <= s - 2 < count:
-            back_tokens(s - 2)
-        if 0 <= s - 3 < count:
-            finish(s - 3)
+    run_in_order(len(BACK_PIECES), (back_rows, back_slots, back_tokens, finish), BACK_LAGS, {})
 
     for p in (0, 1):
         await_bytes(metas[p].at[0:48, :], send_sem.at[p])
@@ -422,9 +419,9 @@
         buf(D, HW),
         buf(D, HW),
         buf(HW, D),
-        buf(TOK, 128),
-        buf(64, 128),
-        buf(64, 128),
+        buf(TOK, 256),
+        buf(64, 256),
+        buf(64, 256),
         buf(128, 128),
         buf(128, 128),
         buf(128, 128),
@@ -445,6 +442,9 @@
         buf(128, 128),
         buf(128, 128),
         buf(128, 128),
+        buf(128, 128),
+        buf(128, 128),
+        buf(128, 128),
         pltpu.VMEM((128, HW), F32),
         pltpu.VMEM((128, HW), F32),
         pltpu.VMEM((128, HW), F32),
@@ -454,7 +454,6 @@
         buf(128, D),
         buf(128, D),
         buf(128, D),
-        buf(64, D),
         buf(64, D),
         dma((3, n_out)),
         dma((4,)),
@@ -466,16 +465,17 @@
         dma((n_back,)),
         dma((12,)),
     ]
-    return pl.pallas_call(
+    parts = pl.pallas_call(
         kernel,
-        out_shape=jax.ShapeDtypeStruct((TOK, D), BF16),
+        out_shape=jax.ShapeDtypeStruct((4 * TOK, D), BF16),
         in_specs=[anywhere, anywhere, vmem, vmem, anywhere, anywhere, anywhere],
-        out_specs=vmem,
+        out_specs=anywhere,
         scratch_shapes=scratch,
         compiler_params=pltpu.CompilerParams(
             collective_id=0, has_side_effects=True, vmem_limit_bytes=60 * 2**20
         ),
-    )(layer_input, grad_output, expert_ids, route_weights, w_gate, w_up, w_down)
+    )(layer_input, grad_output, expert_ids.T, route_weights.T, w_gate, w_up, w_down)
+    return jnp.sum(parts.reshape(4, TOK, D).astype(F32), axis=0).astype(BF16)
 
 
 def solution(mesh):

time: 76.9 us -> 65.3 us (0.85)
  Pallas kernels: 72.4 us -> 63.4 us
  local copies, waits for them, and re-layouts: 4.25 us -> 0 us
  other arithmetic: 0 us -> 1.76 us
    pallas_call x1, Pallas kernels: 72.4 us -> 63.4 us  [local(): pl.pallas_call(kernel, out_shape=jax.ShapeDtypeStruct((4 * TOK, D), BF16)...]
    unnamed x3 -> x0, local copies, waits for them, and re-layouts: 4.25 us -> none
    reduce_sum x0 -> x1, other arithmetic: none -> 1.76 us  [local(): return jnp.sum(parts.reshape(4, TOK, D).astype(F32), axis=0).astype(BF16)]
where the time goes in v2:
time: 65.3 us; the launch traced here: 65.1 us
  Pallas kernels  63.4 us (97%)
  other arithmetic  1.76 us (3%)
    pallas_call x1, Pallas kernels, local(): pl.pallas_call(kernel, out_shape=jax.ShapeDtypeStruct((4 * TOK, D), BF16)...  63.4 us
    reduce_sum x1, other arithmetic, local(): return jnp.sum(parts.reshape(4, TOK, D).astype(F32), axis=0).astype(BF16)  1.76 us

profile of v2, /device:TPU:1, one launch (start us, length us, event | category | flops | bytes accessed | tf_op | source)
XLA Modules:
  0.0 65.1 jit_solution(3767525037811989025)
XLA Ops:
  0.0 63.4 %shard_map.73 = bf16[64,3584]{1,0:T(8,128)(2,1)} custom-call(bf16[16,3584]{1,0:T(8,128)(2,1)} %x_in.1, bf16[16,3584]{1,0:T(8,128)(2,1)} %g_in.1, s32[8,16]{1,0:T(8,128)} %bitcast.4, bf16[8,16]{1,0:T(8,128)(2,1)} %bitcast.5, bf16[1,3584,1024]{2,1,0:T(8,128)(2,1)} %wg_hbm.1, bf16[1,3584,1024]{2,1,0:T(8,128)(2,1)} %wu_hbm.1, bf16[1,1024,3584]{2,1,0:T(8,128)(2,1)} %wd_hbm.1), custom_call_target="tpu_custom_call" | custom-call | tf_op jit(solution)/shard_map/pallas_call | solution.py:468
  63.4 1.8 %reduce_sum.12 = bf16[16,3584]{1,0:T(8,128)(2,1)} reduce(bf16[4,16,3584]{2,1,0:T(8,128)(2,1)} %bitcast.3, bf16[]{:T(256)} %constant.2.clone.1), dimensions={0}, to_apply=%region_0.0 | reduce | flops 172032 | bytes 573442 | tf_op jit(solution)/shard_map/reduce_sum | solution.py:478

commit v3 on v2

--- a/solution.py
+++ b/solution.py
@@ -14,7 +14,8 @@
 TOK = 16
 OUT_CUTS = (512, 768, 768, 768, 512, 256)
 BACK_CUTS = (512,) * 7
-HB = 512
+HB = 1024
+RB = 512
 NB = 256
 
 
@@ -27,7 +28,7 @@
 BACK_PIECES = pieces(BACK_CUTS)
 
 
-OUT_LAGS = (-3, 0, 2, 4)
+OUT_LAGS = (-3, 0, 1, 3)
 BACK_LAGS = (0, 4, 7, 10)
 
 
@@ -344,9 +345,9 @@
         start, width = BACK_PIECES[i]
         cut = pl.ds(start, width)
 
-        @pl.loop(0, width // NB)
+        @pl.loop(0, width // RB)
         def _(n):
-            block = rows(start + n * NB, NB)
+            block = rows(start + n * RB, RB)
             total = dot_t(d_gate[...], wg[block, :]) + dot_t(d_up[...], wu[block, :])
             y_s[:, block] = total.astype(BF16)
 

time: 65.3 us -> 64.9 us (level)
  no operation moved by 1% of the time
where the time goes in v3:
time: 64.9 us; the launch traced here: 64.7 us
  Pallas kernels  62.9 us (97%)
  other arithmetic  1.76 us (3%)
    pallas_call x1, Pallas kernels, local(): pl.pallas_call(kernel, out_shape=jax.ShapeDtypeStruct((4 * TOK, D), BF16)...  62.9 us
    reduce_sum x1, other arithmetic, local(): return jnp.sum(parts.reshape(4, TOK, D).astype(F32), axis=0).astype(BF16)  1.76 us

profile of v3, /device:TPU:1, one launch (start us, length us, event | category | flops | bytes accessed | tf_op | source)
XLA Modules:
  0.0 64.7 jit_solution(16263838812820631047)
XLA Ops:
  0.0 62.9 %shard_map.73 = bf16[64,3584]{1,0:T(8,128)(2,1)} custom-call(bf16[16,3584]{1,0:T(8,128)(2,1)} %x_in.1, bf16[16,3584]{1,0:T(8,128)(2,1)} %g_in.1, s32[8,16]{1,0:T(8,128)} %bitcast.4, bf16[8,16]{1,0:T(8,128)(2,1)} %bitcast.5, bf16[1,3584,1024]{2,1,0:T(8,128)(2,1)} %wg_hbm.1, bf16[1,3584,1024]{2,1,0:T(8,128)(2,1)} %wu_hbm.1, bf16[1,1024,3584]{2,1,0:T(8,128)(2,1)} %wd_hbm.1), custom_call_target="tpu_custom_call" | custom-call | tf_op jit(solution)/shard_map/pallas_call | solution.py:469
  63.0 1.8 %reduce_sum.12 = bf16[16,3584]{1,0:T(8,128)(2,1)} reduce(bf16[4,16,3584]{2,1,0:T(8,128)(2,1)} %bitcast.3, bf16[]{:T(256)} %constant.2.clone.1), dimensions={0}, to_apply=%region_0.0 | reduce | flops 172032 | bytes 573442 | tf_op jit(solution)/shard_map/reduce_sum | solution.py:479

commit v4 on v3

--- a/solution.py
+++ b/solution.py
@@ -172,7 +172,9 @@
         )
 
     barrier = pltpu.get_barrier_semaphore()
-    partners = [d for _, d in zc_plane] + [d for _, d in yc_plane[:-1]] + [d for _, d in x_line]
+    pairs = zip(zc_plane[:-1], yc_plane[:-1])
+    partners = [d for pair in pairs for _, d in pair] + [zc_plane[-1][1]]
+    partners = [x_line[0][1]] + partners + [d for _, d in x_line[1:]]
     for target in partners:
         pl.semaphore_signal(barrier, inc=1, device_id=target, device_id_type=MESH)
 

time: 64.9 us -> 64.9 us (level)
  no operation moved by 1% of the time
where the time goes in v4:
time: 64.9 us; the launch traced here: 64.7 us
  Pallas kernels  62.9 us (97%)
  other arithmetic  1.76 us (3%)
    pallas_call x1, Pallas kernels, local(): pl.pallas_call(kernel, out_shape=jax.ShapeDtypeStruct((4 * TOK, D), BF16)...  62.9 us
    reduce_sum x1, other arithmetic, local(): return jnp.sum(parts.reshape(4, TOK, D).astype(F32), axis=0).astype(BF16)  1.76 us

profile of v4, /device:TPU:1, one launch (start us, length us, event | category | flops | bytes accessed | tf_op | source)
XLA Modules:
  0.0 64.7 jit_solution(16266799750363942322)
XLA Ops:
  0.0 62.9 %shard_map.73 = bf16[64,3584]{1,0:T(8,128)(2,1)} custom-call(bf16[16,3584]{1,0:T(8,128)(2,1)} %x_in.1, bf16[16,3584]{1,0:T(8,128)(2,1)} %g_in.1, s32[8,16]{1,0:T(8,128)} %bitcast.4, bf16[8,16]{1,0:T(8,128)(2,1)} %bitcast.5, bf16[1,3584,1024]{2,1,0:T(8,128)(2,1)} %wg_hbm.1, bf16[1,3584,1024]{2,1,0:T(8,128)(2,1)} %wu_hbm.1, bf16[1,1024,3584]{2,1,0:T(8,128)(2,1)} %wd_hbm.1), custom_call_target="tpu_custom_call" | custom-call | tf_op jit(solution)/shard_map/pallas_call | solution.py:471
  63.0 1.8 %reduce_sum.12 = bf16[16,3584]{1,0:T(8,128)(2,1)} reduce(bf16[4,16,3584]{2,1,0:T(8,128)(2,1)} %bitcast.3, bf16[]{:T(256)} %constant.2.clone.1), dimensions={0}, to_apply=%region_0.0 | reduce | flops 172032 | bytes 573442 | tf_op jit(solution)/shard_map/reduce_sum | solution.py:481
